TPU v7x, 32 devices: a whole 2x2x4 slice. The times are simulated.
32 devices in a mesh: row: 2 (over y), col: 4 (over x, core), rep: 4 (over z).
Axes of the slice: x: 2, y: 2, z: 4, core: 2. Of those that a mesh axis runs over, the one named last changes fastest.
Arguments:
- amplitudes: bfloat16 [384, 100, 1024], P(('row', 'col'), 'rep'), may hold values from -6 to 6
- integrals: bfloat16 [100, 1024, 256], P('rep', 'col', 'row'), may hold values from -0.02734375 to 0.02734375
Outputs:
- cycle: float32 [384, 256], P('row', ('col', 'rep'))
All inputs are finite; a program needn't handle non-finite values.
Results may differ from a plain program's by a relative error of at most 0.0003.
Values may be sent and summed in bfloat16 or wider, within the bound.
A program may use at most 64 MiB of HBM per device.

v0:
```python
import jax
import jax.numpy as jnp
from jax import lax
from jax.sharding import PartitionSpec as P


def local(amplitudes, integrals):
    remapped = lax.all_to_all(amplitudes, "col", split_axis=2, concat_axis=0, tiled=True)
    row_count = remapped.shape[0]
    flattened = remapped.reshape(row_count, -1)
    columns = lax.all_gather(integrals, "row", axis=2, tiled=True).reshape(flattened.shape[1], -1)
    partial_value = jnp.dot(flattened, columns, preferred_element_type=jnp.float32)
    summed = lax.psum_scatter(partial_value, ("col", "rep"), scatter_dimension=1, tiled=True)
    return summed


def solution(mesh):
    return jax.shard_map(
        local,
        mesh=mesh,
        in_specs=(P(("row", "col"), "rep", None), P("rep", "col", "row")),
        out_specs=P("row", ("col", "rep")),
        check_vma=False,
    )
```

profile of v0, /device:TPU:0, one launch (start us, length us, event | category | flops | bytes accessed | tf_op | source)
XLA Modules:
  0.0 156.3 jit_solution(14165026655411933823)
XLA Ops:
  6.5 0.0 all-gather.2.cloned.1.call-start
  6.5 0.7 all-gather.2.cloned.1.call-update
  7.3 0.0 reduce-scatter.2.cloned.1.call-start
  7.3 12.9 %copy.4 = bf16[48,25,1024]{0,1,2:T(8,128)(2,1)} copy(bf16[48,25,1024]{2,0,1:T(8,128)(2,1)} %param.2) | data formatting | bytes 4915200 | tf_op args[0]
  20.2 10.7 %reshape.9 = bf16[4,2,153600]{2,1,0:T(2,128)(2,1)S(1)} reshape(bf16[1024,25,48]{2,1,0:T(8,128)(2,1)} %bitcast.11) | data formatting | bytes 4915200
  30.9 33.6 %all_to_all.15 = bf16[4,2,153600]{2,1,0:T(2,128)(2,1)} all-to-all(bf16[4,2,153600]{2,1,0:T(2,128)(2,1)S(1)} %reshape.9), channel_id=1, replica_groups=mesh['row'=2,'col'=4,'rep'=4] {'col'}, dimensions={0} | all-to-all | bytes 4915200 | tf_op jit(solution)/shard_map/all_to_all | solution.py:8
  64.5 8.6 %reshape.10 = bf16[1024,25,48]{2,1,0:T(8,128)(2,1)} reshape(bf16[4,2,153600]{2,1,0:T(2,128)(2,1)} %all_to_all.15) | data formatting | bytes 4915200
  73.2 11.9 %copy.5 = bf16[48,25,4,256]{3,1,0,2:T(8,128)(2,1)S(1)} copy(bf16[48,25,4,256]{0,1,3,2:T(8,128)(2,1)} %bitcast.10) | data formatting | bytes 4915200 | tf_op jit(solution)/shard_map/all_to_all | solution.py:8
  85.0 3.2 %copy.6 = bf16[24,8,25,256]{3,1,2,0:T(8,128)(2,1)} copy(bf16[24,8,25,256]{3,2,1,0:T(8,128)(2,1)S(1)} %bitcast.12) | data formatting | bytes 4915200
  88.3 0.0 all-gather.2.cloned.1.call-done
  88.3 4.8 %fusion = f32[192,256]{0,1:T(8,128)} fusion(bf16[192,6400]{1,0:T(8,128)(2,1)} %bitcast.13, bf16[6400,256]{1,0:T(8,128)(2,1)} %bitcast.14), kind=kOutput, calls=%fused_computation | convolution fusion | flops 629145600 | bytes 5931008 | tf_op jit(solution)/shard_map/dot_general | solution.py:12
  93.0 0.0 reduce-scatter.2.cloned.1.call-update
  93.1 56.4 %reduce-scatter.2.cloned.1.call-done = f32[192,16]{0,1:T(8,128)} async-done(((f32[192,256]{0,1:T(8,128)}), f32[192,16]{0,1:T(8,128)}) %reduce-scatter.2.cloned.1.call-update) | async-done | bytes 12304 | tf_op jit(solution)/shard_map/reduce_scatter | solution.py:13
Async XLA Ops:
  6.5 81.7 %all-gather.2.cloned.1.call-start = ((), (), s32[]{:S(2)}) async-start(), calls=%async_computation.2 | async-start | bytes 4915200 | tf_op jit(solution)/shard_map/all_gather | solution.py:11
  7.3 142.2 %reduce-scatter.2.cloned.1.call-start = ((), (), s32[]{:S(2)}) async-start(), calls=%async_computation.3 | async-start | bytes 278528 | tf_op jit(solution)/shard_map/reduce_scatter | solution.py:13
Sparse Core Ops, SparseCore 0:
  8.9 49.0 all-gather.1
  93.2 56.1 reduce-scatter.1
where the time goes:
time: 157 us; the launch traced here: 156 us
  waiting for transfers between devices  57.1 us (36%)
  local copies, waits for them, and re-layouts  47.3 us (30%)
  blocking collectives  33.6 us (21%)
  between operations  13.4 us (9%)
  matrix products  4.77 us (3%)
    reduce_scatter x1, waiting for transfers between devices, local(): lax.psum_scatter(partial_value, ('col', 'rep'), scatter_dimension=1, tile...  56.4 us
    unnamed x4, local copies, waits for them, and re-layouts  35.4 us
    all_to_all x1, blocking collectives, local(): lax.all_to_all(amplitudes, 'col', split_axis=2, concat_axis=0, tiled=True)  33.6 us
    all_to_all x1, local copies, waits for them, and re-layouts, local(): lax.all_to_all(amplitudes, 'col', split_axis=2, concat_axis=0, tiled=True)  11.9 us
    dot_general x1, matrix products, local(): jnp.dot(flattened, columns, preferred_element_type=jnp.float32)  4.77 us
  transfers between devices with their start and end apart: 2, of which 1 were waited for; matrix products, arithmetic and copies ran while one was open for 30% of the time, Pallas kernels for 0%

commit v1 on v0

v1 whole, which is shorter than its diff:
```python
import functools

import jax
import jax.numpy as jnp
from jax import lax
from jax.experimental import pallas as pl
from jax.experimental.pallas import tpu as pltpu
from jax.sharding import PartitionSpec as P

MESH = pl.DeviceIdType.MESH


def chunk_bounds(depth):
    count = min(5, depth)
    edges = [depth * i // count for i in range(count + 1)]
    return list(zip(edges[:-1], edges[1:]))


def kernel(sizes, split, a_ref, b_ref, o_ref, a_buf, b_buf, parts, inbox,
           a_send, a_recv, b_send, b_recv, p_send, p_recv, own_sem):
    rows, cols, reps = sizes
    row, col, rep = lax.axis_index("row"), lax.axis_index("col"), lax.axis_index("rep")
    group = cols * reps
    me = col * reps + rep
    depth, height, width = a_buf.shape[1:]
    lanes = b_buf.shape[3]
    share = parts.shape[1]
    per = lanes // share
    total_rows = cols * height
    bounds = chunk_bounds(depth)

    def row_at(d):
        return lax.rem(row + d, rows)

    def col_at(d):
        return lax.rem(col + d, cols)

    barrier = pltpu.get_barrier_semaphore()
    for d in range(1, rows):
        pl.semaphore_signal(barrier, inc=1, device_id={"row": row_at(d)}, device_id_type=MESH)
    for d in range(1, group):
        other = lax.rem(me + d, group)
        pl.semaphore_signal(barrier, inc=1, device_id={"col": other // reps, "rep": lax.rem(other, reps)},
                            device_id_type=MESH)

    def piece(lo, hi, owner):
        if split:
            return a_ref.at[owner, lo:hi]
        return a_ref.at[lo:hi, :, pl.ds(pl.multiple_of(owner * width, width), width)]

    own_a = pltpu.make_async_copy(piece(0, depth, col), a_buf.at[col], own_sem.at[0])
    own_b = pltpu.make_async_copy(b_ref, b_buf.at[row], own_sem.at[1])
    own_a.start()
    own_b.start()
    pl.semaphore_wait(barrier, rows - 1 + group - 1)

    a_copies, b_copies = [], []
    for g, (lo, hi) in enumerate(bounds):
        b_copies.append([])
        for d in range(1, rows):
            copy = pltpu.make_async_remote_copy(
                src_ref=b_ref.at[lo:hi], dst_ref=b_buf.at[row, lo:hi],
                send_sem=b_send.at[d - 1, g], recv_sem=b_recv.at[d - 1, g],
                device_id={"row": row_at(d)}, device_id_type=MESH)
            copy.start()
            b_copies[-1].append(copy)
        a_copies.append([])
        for d in range(1, cols):
            copy = pltpu.make_async_remote_copy(
                src_ref=piece(lo, hi, col_at(d)), dst_ref=a_buf.at[col, lo:hi],
                send_sem=a_send.at[d - 1, g], recv_sem=a_recv.at[d - 1, g],
                device_id={"col": col_at(d)}, device_id_type=MESH)
            copy.start()
            a_copies[-1].append(copy)

    def product(lo, hi, source):
        left = jnp.concatenate(
            [jnp.concatenate([a_buf[c, k] for c in range(cols)], axis=0) for k in range(lo, hi)], axis=1)
        right = jnp.concatenate([b_buf[source, k] for k in range(lo, hi)], axis=0)
        return jnp.dot(left, right, preferred_element_type=jnp.float32)

    def part_copy(owner):
        return pltpu.make_async_remote_copy(
            src_ref=parts.at[owner], dst_ref=inbox.at[me],
            send_sem=p_send.at[owner], recv_sem=p_recv.at[me],
            device_id={"col": owner // reps, "rep": lax.rem(owner, reps)}, device_id_type=MESH)

    def hand_out(source, value):
        parts[pl.ds(source * per, per)] = value.T.reshape(per, share, total_rows)
        for i in range(per):
            owner = source * per + i

            @pl.when(owner != me)
            def _():
                part_copy(owner).start()

    own_a.wait()
    own_b.wait()
    value = None
    for g, (lo, hi) in enumerate(bounds):
        for copy in a_copies[g]:
            copy.wait_recv()
        term = product(lo, hi, row)
        value = term if value is None else value + term
    hand_out(row, value)

    for d in range(1, rows):
        source = lax.rem(row + rows - d, rows)
        value = None
        for g, (lo, hi) in enumerate(bounds):
            b_copies[g][d - 1].wait_recv()
            term = product(lo, hi, source)
            value = term if value is None else value + term
        hand_out(source, value)

    result = parts[me]
    for d in range(1, group):
        source = lax.rem(me + d, group)
        pltpu.make_async_remote_copy(
            src_ref=parts.at[source], dst_ref=inbox.at[source],
            send_sem=p_send.at[source], recv_sem=p_recv.at[source],
            device_id={"col": source // reps, "rep": lax.rem(source, reps)}, device_id_type=MESH).wait_recv()
        result = result + inbox[source]
    o_ref[...] = result

    for copies in a_copies + b_copies:
        for copy in copies:
            copy.wait_send()
    for d in range(1, group):
        part_copy(lax.rem(me + d, group)).wait_send()


def local(sizes, amplitudes, integrals):
    rows, cols, reps = sizes
    height, depth, virtuals = amplitudes.shape
    width, lanes = integrals.shape[1:]
    group = cols * reps
    share = rows * lanes // group
    chunks = len(chunk_bounds(depth))
    split = width % 128 != 0
    blocks = jnp.transpose(amplitudes, (1, 0, 2))
    if split:
        blocks = jnp.transpose(blocks.reshape(depth, height, cols, width), (2, 0, 1, 3))
    dma = pltpu.SemaphoreType.DMA
    summed = pl.pallas_call(
        functools.partial(kernel, sizes, split),
        out_shape=jax.ShapeDtypeStruct((share, cols * height), jnp.float32),
        in_specs=[pl.BlockSpec(memory_space=pl.ANY)] * 2,
        out_specs=pl.BlockSpec(memory_space=pltpu.VMEM),
        scratch_shapes=[
            pltpu.VMEM((cols, depth, height, width), amplitudes.dtype),
            pltpu.VMEM((rows, depth, width, lanes), integrals.dtype),
            pltpu.VMEM((group, share, cols * height), jnp.float32),
            pltpu.VMEM((group, share, cols * height), jnp.float32),
            dma((max(cols - 1, 1), chunks)),
            dma((max(cols - 1, 1), chunks)),
            dma((max(rows - 1, 1), chunks)),
            dma((max(rows - 1, 1), chunks)),
            dma((group,)),
            dma((group,)),
            dma((2,)),
        ],
        compiler_params=pltpu.CompilerParams(
            collective_id=0, has_side_effects=True, vmem_limit_bytes=56 * 1024 * 1024),
        cost_estimate=pl.CostEstimate(
            flops=2 * cols * height * rows * lanes * depth * width,
            bytes_accessed=2 * (amplitudes.size + integrals.size), transcendentals=0),
    )(blocks, integrals)
    return summed.T


def solution(mesh):
    sizes = (mesh.shape["row"], mesh.shape["col"], mesh.shape["rep"])
    return jax.shard_map(
        functools.partial(local, sizes),
        mesh=mesh,
        in_specs=(P(("row", "col"), "rep", None), P("rep", "col", "row")),
        out_specs=P("row", ("col", "rep")),
        check_vma=False,
    )
```

time: 157 us -> 49.7 us (0.32)
  waiting for transfers between devices: 57.1 us -> 0 us
  Pallas kernels: 0 us -> 48.2 us
  local copies, waits for them, and re-layouts: 47.3 us -> 1.32 us
  blocking collectives: 33.6 us -> 0 us
  between operations: 13.4 us -> 0.01 us
  matrix products: 4.77 us -> 0 us
    reduce_scatter x1 -> x0, waiting for transfers between devices: 56.4 us -> none  [local(): lax.psum_scatter(partial_value, ('col', 'rep'), scatter_dimension=1, tile...]
    pallas_call x0 -> x1, Pallas kernels: none -> 48.2 us  [local(): pl.pallas_call(functools.partial(kernel, sizes, split), out_shape=jax.Sha...]
    unnamed x4 -> x1, local copies, waits for them, and re-layouts: 35.4 us -> 1.32 us
    all_to_all x1 -> x0, blocking collectives: 33.6 us -> none  [local(): lax.all_to_all(amplitudes, 'col', split_axis=2, concat_axis=0, tiled=True)]
    all_to_all x1 -> x0, local copies, waits for them, and re-layouts: 11.9 us -> none  [local(): lax.all_to_all(amplitudes, 'col', split_axis=2, concat_axis=0, tiled=True)]
    dot_general x1 -> x0, matrix products: 4.77 us -> none  [local(): jnp.dot(flattened, columns, preferred_element_type=jnp.float32)]
  transfers between devices with their start and end apart: 2 -> 0, of which waited for: 1 -> 0; matrix products, arithmetic and copies ran while one was open for 30% -> 0% of each run, Pallas kernels for 0% -> 0%
where the time goes in v1:
time: 49.7 us; the launch traced here: 49.5 us
  Pallas kernels  48.2 us (97%)
  local copies, waits for them, and re-layouts  1.32 us (3%)
    pallas_call x1, Pallas kernels, local(): pl.pallas_call(functools.partial(kernel, sizes, split), out_shape=jax.Sha...  48.2 us
    unnamed x1, local copies, waits for them, and re-layouts  1.32 us

profile of v1, /device:TPU:0, one launch (start us, length us, event | category | flops | bytes accessed | tf_op | source)
XLA Modules:
  0.0 49.5 jit_solution(13668594302020888235)
XLA Ops:
  0.0 48.2 %shard_map.28 = f32[16,192]{1,0:T(8,128)} custom-call(bf16[25,48,1024]{2,1,0:T(8,128)(2,1)} %bitcast.2, bf16[25,256,128]{2,1,0:T(8,128)(2,1)} %b_ref.1), custom_call_target="tpu_custom_call" | custom-call | flops 629145600 | bytes 4096000 | tf_op jit(solution)/shard_map/pallas_call | solution.py:145
  48.2 1.3 %copy.4 = f32[192,16]{0,1:T(8,128)} copy(f32[192,16]{0,1:T(8,128)} %bitcast.3) | data formatting | bytes 24576

commit v2 on v1

--- a/solution.py
+++ b/solution.py
@@ -11,8 +11,7 @@
 
 
 def chunk_bounds(depth):
-    count = min(5, depth)
-    edges = [depth * i // count for i in range(count + 1)]
+    edges = sorted({0, depth * 6 // 25, depth * 12 // 25, depth * 18 // 25, depth * 22 // 25, depth - 1, depth})
     return list(zip(edges[:-1], edges[1:]))
 
 
@@ -81,8 +80,8 @@
 
     def part_copy(owner):
         return pltpu.make_async_remote_copy(
-            src_ref=parts.at[owner], dst_ref=inbox.at[me],
-            send_sem=p_send.at[owner], recv_sem=p_recv.at[me],
+            src_ref=parts.at[owner], dst_ref=inbox.at[lax.rem(owner - me + group, group) - 1],
+            send_sem=p_send, recv_sem=p_recv,
             device_id={"col": owner // reps, "rep": lax.rem(owner, reps)}, device_id_type=MESH)
 
     def hand_out(source, value):
@@ -104,30 +103,33 @@
         value = term if value is None else value + term
     hand_out(row, value)
 
+    for copies in a_copies:
+        for copy in copies:
+            copy.wait_send()
+
     for d in range(1, rows):
         source = lax.rem(row + rows - d, rows)
         value = None
         for g, (lo, hi) in enumerate(bounds):
+            if g > 0:
+                b_copies[g - 1][d - 1].wait_send()
             b_copies[g][d - 1].wait_recv()
             term = product(lo, hi, source)
             value = term if value is None else value + term
         hand_out(source, value)
 
+    pieces = pltpu.make_async_remote_copy(
+        src_ref=parts.at[0:group - 1], dst_ref=inbox, send_sem=p_send, recv_sem=p_recv,
+        device_id={"col": col_at(1)}, device_id_type=MESH)
+    pieces.wait_recv()
     result = parts[me]
-    for d in range(1, group):
-        source = lax.rem(me + d, group)
-        pltpu.make_async_remote_copy(
-            src_ref=parts.at[source], dst_ref=inbox.at[source],
-            send_sem=p_send.at[source], recv_sem=p_recv.at[source],
-            device_id={"col": source // reps, "rep": lax.rem(source, reps)}, device_id_type=MESH).wait_recv()
-        result = result + inbox[source]
+    for i in range(group - 1):
+        result = result + inbox[i]
     o_ref[...] = result
 
-    for copies in a_copies + b_copies:
-        for copy in copies:
-            copy.wait_send()
-    for d in range(1, group):
-        part_copy(lax.rem(me + d, group)).wait_send()
+    for copy in b_copies[-1]:
+        copy.wait_send()
+    pieces.wait_send()
 
 
 def local(sizes, amplitudes, integrals):
@@ -151,13 +153,13 @@
             pltpu.VMEM((cols, depth, height, width), amplitudes.dtype),
             pltpu.VMEM((rows, depth, width, lanes), integrals.dtype),
             pltpu.VMEM((group, share, cols * height), jnp.float32),
-            pltpu.VMEM((group, share, cols * height), jnp.float32),
+            pltpu.VMEM((group - 1, share, cols * height), jnp.float32),
             dma((max(cols - 1, 1), chunks)),
             dma((max(cols - 1, 1), chunks)),
             dma((max(rows - 1, 1), chunks)),
             dma((max(rows - 1, 1), chunks)),
-            dma((group,)),
-            dma((group,)),
+            dma,
+            dma,
             dma((2,)),
         ],
         compiler_params=pltpu.CompilerParams(

time: 49.7 us -> 49.4 us (level)
  no operation moved by 1% of the time
where the time goes in v2:
time: 49.4 us; the launch traced here: 49.2 us
  Pallas kernels  47.8 us (97%)
  local copies, waits for them, and re-layouts  1.32 us (3%)
    pallas_call x1, Pallas kernels, local(): pl.pallas_call(functools.partial(kernel, sizes, split), out_shape=jax.Sha...  47.8 us
    unnamed x1, local copies, waits for them, and re-layouts  1.32 us

profile of v2, /device:TPU:0, one launch (start us, length us, event | category | flops | bytes accessed | tf_op | source)
XLA Modules:
  0.0 49.2 jit_solution(11242004180332958774)
XLA Ops:
  0.0 47.8 %shard_map.28 = f32[16,192]{1,0:T(8,128)} custom-call(bf16[25,48,1024]{2,1,0:T(8,128)(2,1)} %bitcast.2, bf16[25,256,128]{2,1,0:T(8,128)(2,1)} %b_ref.1), custom_call_target="tpu_custom_call" | custom-call | flops 629145600 | bytes 4096000 | tf_op jit(solution)/shard_map/pallas_call | solution.py:147
  47.8 1.3 %copy.4 = f32[192,16]{0,1:T(8,128)} copy(f32[192,16]{0,1:T(8,128)} %bitcast.3) | data formatting | bytes 24576

commit v3 on v2

--- a/solution.py
+++ b/solution.py
@@ -49,8 +49,6 @@
 
     own_a = pltpu.make_async_copy(piece(0, depth, col), a_buf.at[col], own_sem.at[0])
     own_b = pltpu.make_async_copy(b_ref, b_buf.at[row], own_sem.at[1])
-    own_a.start()
-    own_b.start()
     pl.semaphore_wait(barrier, rows - 1 + group - 1)
 
     a_copies, b_copies = [], []
@@ -63,6 +61,7 @@
                 device_id={"row": row_at(d)}, device_id_type=MESH)
             copy.start()
             b_copies[-1].append(copy)
+    for g, (lo, hi) in enumerate(bounds):
         a_copies.append([])
         for d in range(1, cols):
             copy = pltpu.make_async_remote_copy(
@@ -71,6 +70,9 @@
                 device_id={"col": col_at(d)}, device_id_type=MESH)
             copy.start()
             a_copies[-1].append(copy)
+
+    own_a.start()
+    own_b.start()
 
     def product(lo, hi, source):
         left = jnp.concatenate(

time: 49.4 us -> 49.4 us (level)
  no operation moved by 1% of the time
where the time goes in v3:
time: 49.4 us; the launch traced here: 49.2 us
  Pallas kernels  47.8 us (97%)
  local copies, waits for them, and re-layouts  1.32 us (3%)
    pallas_call x1, Pallas kernels, local(): pl.pallas_call(functools.partial(kernel, sizes, split), out_shape=jax.Sha...  47.8 us
    unnamed x1, local copies, waits for them, and re-layouts  1.32 us

profile of v3, /device:TPU:0, one launch (start us, length us, event | category | flops | bytes accessed | tf_op | source)
XLA Modules:
  0.0 49.2 jit_solution(15968048574445680599)
XLA Ops:
  0.0 47.8 %shard_map.28 = f32[16,192]{1,0:T(8,128)} custom-call(bf16[25,48,1024]{2,1,0:T(8,128)(2,1)} %bitcast.2, bf16[25,256,128]{2,1,0:T(8,128)(2,1)} %b_ref.1), custom_call_target="tpu_custom_call" | custom-call | flops 629145600 | bytes 4096000 | tf_op jit(solution)/shard_map/pallas_call | solution.py:149
  47.8 1.3 %copy.4 = f32[192,16]{0,1:T(8,128)} copy(f32[192,16]{0,1:T(8,128)} %bitcast.3) | data formatting | bytes 24576

commit v4 on v3

--- a/solution.py
+++ b/solution.py
@@ -15,17 +15,12 @@
     return list(zip(edges[:-1], edges[1:]))
 
 
-def kernel(sizes, split, a_ref, b_ref, o_ref, a_buf, b_buf, parts, inbox,
-           a_send, a_recv, b_send, b_recv, p_send, p_recv, own_sem):
+def kernel(sizes, split, a_ref, b_ref, o_ref, a_buf, b_buf, parts, z_inbox, mid, c_inbox, mine,
+           a_send, a_recv, b_send, b_recv, z_send, z_recv, c_send, c_recv, own_sem):
     rows, cols, reps = sizes
     row, col, rep = lax.axis_index("row"), lax.axis_index("col"), lax.axis_index("rep")
-    group = cols * reps
-    me = col * reps + rep
     depth, height, width = a_buf.shape[1:]
-    lanes = b_buf.shape[3]
-    share = parts.shape[1]
-    per = lanes // share
-    total_rows = cols * height
+    near, share, total_rows = parts.shape[2:]
     bounds = chunk_bounds(depth)
 
     def row_at(d):
@@ -33,14 +28,17 @@
 
     def col_at(d):
         return lax.rem(col + d, cols)
+
+    def rep_at(d):
+        return lax.rem(rep + d, reps)
 
     barrier = pltpu.get_barrier_semaphore()
     for d in range(1, rows):
         pl.semaphore_signal(barrier, inc=1, device_id={"row": row_at(d)}, device_id_type=MESH)
-    for d in range(1, group):
-        other = lax.rem(me + d, group)
-        pl.semaphore_signal(barrier, inc=1, device_id={"col": other // reps, "rep": lax.rem(other, reps)},
-                            device_id_type=MESH)
+    for d in range(1, cols):
+        pl.semaphore_signal(barrier, inc=1, device_id={"col": col_at(d)}, device_id_type=MESH)
+    for d in range(1, reps):
+        pl.semaphore_signal(barrier, inc=1, device_id={"rep": rep_at(d)}, device_id_type=MESH)
 
     def piece(lo, hi, owner):
         if split:
@@ -49,7 +47,7 @@
 
     own_a = pltpu.make_async_copy(piece(0, depth, col), a_buf.at[col], own_sem.at[0])
     own_b = pltpu.make_async_copy(b_ref, b_buf.at[row], own_sem.at[1])
-    pl.semaphore_wait(barrier, rows - 1 + group - 1)
+    pl.semaphore_wait(barrier, rows + cols + reps - 3)
 
     a_copies, b_copies = [], []
     for g, (lo, hi) in enumerate(bounds):
@@ -80,20 +78,38 @@
         right = jnp.concatenate([b_buf[source, k] for k in range(lo, hi)], axis=0)
         return jnp.dot(left, right, preferred_element_type=jnp.float32)
 
-    def part_copy(owner):
-        return pltpu.make_async_remote_copy(
-            src_ref=parts.at[owner], dst_ref=inbox.at[lax.rem(owner - me + group, group) - 1],
-            send_sem=p_send, recv_sem=p_recv,
-            device_id={"col": owner // reps, "rep": lax.rem(owner, reps)}, device_id_type=MESH)
-
-    def hand_out(source, value):
-        parts[pl.ds(source * per, per)] = value.T.reshape(per, share, total_rows)
-        for i in range(per):
-            owner = source * per + i
-
-            @pl.when(owner != me)
+    def over_reps(h, value):
+        pieces = value.T.reshape(near, reps, share, total_rows)
+        for z in range(reps):
+            parts[h, z] = pieces[:, z]
+        for d in range(1, reps):
+            pltpu.make_async_remote_copy(
+                src_ref=parts.at[h, rep_at(d)], dst_ref=z_inbox.at[h, d - 1],
+                send_sem=z_send.at[h], recv_sem=z_recv.at[h],
+                device_id={"rep": rep_at(d)}, device_id_type=MESH).start()
+
+    def over_cols(h):
+        arrived = pltpu.make_async_remote_copy(
+            src_ref=parts.at[h, 0:reps - 1], dst_ref=z_inbox.at[h], send_sem=z_send.at[h], recv_sem=z_recv.at[h],
+            device_id={"rep": rep_at(1)}, device_id_type=MESH)
+        arrived.wait_recv()
+        total = parts[h, rep]
+        for d in range(reps - 1):
+            total = total + z_inbox[h, d]
+        mid[h] = total
+        for i in range(near):
+            owner = lax.rem(row + rows - h, rows) * near + i
+
+            @pl.when(owner != col)
             def _():
-                part_copy(owner).start()
+                pltpu.make_async_remote_copy(
+                    src_ref=mid.at[h, i], dst_ref=c_inbox.at[lax.rem(owner - col + cols, cols) - 1],
+                    send_sem=c_send, recv_sem=c_recv, device_id={"col": owner}, device_id_type=MESH).start()
+
+            @pl.when(owner == col)
+            def _():
+                mine[...] = mid[h, i]
+        return arrived
 
     own_a.wait()
     own_b.wait()
@@ -103,35 +119,38 @@
             copy.wait_recv()
         term = product(lo, hi, row)
         value = term if value is None else value + term
-    hand_out(row, value)
+    over_reps(0, value)
 
     for copies in a_copies:
         for copy in copies:
             copy.wait_send()
 
+    reduced = []
     for d in range(1, rows):
         source = lax.rem(row + rows - d, rows)
         value = None
         for g, (lo, hi) in enumerate(bounds):
             if g > 0:
                 b_copies[g - 1][d - 1].wait_send()
+            if g == len(bounds) - 1:
+                reduced.append(over_cols(d - 1))
             b_copies[g][d - 1].wait_recv()
             term = product(lo, hi, source)
             value = term if value is None else value + term
-        hand_out(source, value)
-
-    pieces = pltpu.make_async_remote_copy(
-        src_ref=parts.at[0:group - 1], dst_ref=inbox, send_sem=p_send, recv_sem=p_recv,
+        over_reps(d, value)
+    reduced.append(over_cols(rows - 1))
+
+    last = pltpu.make_async_remote_copy(
+        src_ref=c_inbox, dst_ref=c_inbox, send_sem=c_send, recv_sem=c_recv,
         device_id={"col": col_at(1)}, device_id_type=MESH)
-    pieces.wait_recv()
-    result = parts[me]
-    for i in range(group - 1):
-        result = result + inbox[i]
+    last.wait_recv()
+    result = mine[...]
+    for i in range(cols - 1):
+        result = result + c_inbox[i]
     o_ref[...] = result
 
-    for copy in b_copies[-1]:
+    for copy in b_copies[-1] + reduced + [last]:
         copy.wait_send()
-    pieces.wait_send()
 
 
 def local(sizes, amplitudes, integrals):
@@ -140,6 +159,7 @@
     width, lanes = integrals.shape[1:]
     group = cols * reps
     share = rows * lanes // group
+    near = cols // rows
     chunks = len(chunk_bounds(depth))
     split = width % 128 != 0
     blocks = jnp.transpose(amplitudes, (1, 0, 2))
@@ -154,12 +174,17 @@
         scratch_shapes=[
             pltpu.VMEM((cols, depth, height, width), amplitudes.dtype),
             pltpu.VMEM((rows, depth, width, lanes), integrals.dtype),
-            pltpu.VMEM((group, share, cols * height), jnp.float32),
-            pltpu.VMEM((group - 1, share, cols * height), jnp.float32),
+            pltpu.VMEM((rows, reps, near, share, cols * height), jnp.float32),
+            pltpu.VMEM((rows, reps - 1, near, share, cols * height), jnp.float32),
+            pltpu.VMEM((rows, near, share, cols * height), jnp.float32),
+            pltpu.VMEM((cols - 1, share, cols * height), jnp.float32),
+            pltpu.VMEM((share, cols * height), jnp.float32),
             dma((max(cols - 1, 1), chunks)),
             dma((max(cols - 1, 1), chunks)),
             dma((max(rows - 1, 1), chunks)),
             dma((max(rows - 1, 1), chunks)),
+            dma((rows,)),
+            dma((rows,)),
             dma,
             dma,
             dma((2,)),

time: 49.4 us -> 50.9 us (1.030)
  Pallas kernels: 47.8 us -> 49.3 us
    pallas_call x1, Pallas kernels: 47.8 us -> 49.3 us  [local(): pl.pallas_call(functools.partial(kernel, sizes, split), out_shape=jax.Sha...]
where the time goes in v4:
time: 50.9 us; the launch traced here: 50.6 us
  Pallas kernels  49.3 us (97%)
  local copies, waits for them, and re-layouts  1.32 us (3%)
    pallas_call x1, Pallas kernels, local(): pl.pallas_call(functools.partial(kernel, sizes, split), out_shape=jax.Sha...  49.3 us
    unnamed x1, local copies, waits for them, and re-layouts  1.32 us

profile of v4, /device:TPU:0, one launch (start us, length us, event | category | flops | bytes accessed | tf_op | source)
XLA Modules:
  0.0 50.6 jit_solution(12507243326722196831)
XLA Ops:
  0.0 49.3 %shard_map.28 = f32[16,192]{1,0:T(8,128)} custom-call(bf16[25,48,1024]{2,1,0:T(8,128)(2,1)} %bitcast.2, bf16[25,256,128]{2,1,0:T(8,128)(2,1)} %b_ref.1), custom_call_target="tpu_custom_call" | custom-call | flops 629145600 | bytes 4096000 | tf_op jit(solution)/shard_map/pallas_call | solution.py:169
  49.3 1.3 %copy.4 = f32[192,16]{0,1:T(8,128)} copy(f32[192,16]{0,1:T(8,128)} %bitcast.3) | data formatting | bytes 24576

commit v5 on v3

--- a/solution.py
+++ b/solution.py
@@ -13,6 +13,26 @@
 def chunk_bounds(depth):
     edges = sorted({0, depth * 6 // 25, depth * 12 // 25, depth * 18 // 25, depth * 22 // 25, depth - 1, depth})
     return list(zip(edges[:-1], edges[1:]))
+
+
+def packing(share, total_rows):
+    full = total_rows // 128 * 128
+    packed = 2 * (total_rows - full) == 128 and share % 16 == 0
+    return full, packed
+
+
+def pack(value, per, share, full):
+    low = value[:, :full].reshape(per, share, full)
+    high = value[:, full:].reshape(per, 2, share // 2, value.shape[1] - full)
+    high = jnp.concatenate([high[:, 0], high[:, 1]], axis=2)
+    return [low[:, :, i:i + 128] for i in range(0, full, 128)] + [high]
+
+
+def unpack(value, share, full):
+    low = [value[i * share:(i + 1) * share] for i in range(full // 128)]
+    high = value[full // 128 * share:]
+    high = jnp.concatenate([high[:, :64], high[:, 64:]], axis=0)
+    return jnp.concatenate(low + [high], axis=1)
 
 
 def kernel(sizes, split, a_ref, b_ref, o_ref, a_buf, b_buf, parts, inbox,
@@ -23,9 +43,10 @@
     me = col * reps + rep
     depth, height, width = a_buf.shape[1:]
     lanes = b_buf.shape[3]
-    share = parts.shape[1]
-    per = lanes // share
+    per = group // rows
     total_rows = cols * height
+    share = o_ref.shape[0]
+    full, packed = packing(share, total_rows)
     bounds = chunk_bounds(depth)
 
     def row_at(d):
@@ -87,9 +108,15 @@
             device_id={"col": owner // reps, "rep": lax.rem(owner, reps)}, device_id_type=MESH)
 
     def hand_out(source, value):
-        parts[pl.ds(source * per, per)] = value.T.reshape(per, share, total_rows)
+        if packed:
+            start = 0
+            for block in pack(value.T, per, share, full):
+                parts[pl.ds(source * per, per), start:start + block.shape[1]] = block
+                start += block.shape[1]
+        else:
+            parts[pl.ds(source * per, per)] = value.T.reshape(per, share, total_rows)
         for i in range(per):
-            owner = source * per + i
+            owner = source * per + i // reps * reps + lax.rem(2 * reps - 1 - rep - i % reps, reps)
 
             @pl.when(owner != me)
             def _():
@@ -127,7 +154,7 @@
     result = parts[me]
     for i in range(group - 1):
         result = result + inbox[i]
-    o_ref[...] = result
+    o_ref[...] = unpack(result, share, full) if packed else result
 
     for copy in b_copies[-1]:
         copy.wait_send()
@@ -140,6 +167,9 @@
     width, lanes = integrals.shape[1:]
     group = cols * reps
     share = rows * lanes // group
+    tile = (share, cols * height)
+    if packing(*tile)[1]:
+        tile = (share * cols * height // 128, 128)
     chunks = len(chunk_bounds(depth))
     split = width % 128 != 0
     blocks = jnp.transpose(amplitudes, (1, 0, 2))
@@ -154,8 +184,8 @@
         scratch_shapes=[
             pltpu.VMEM((cols, depth, height, width), amplitudes.dtype),
             pltpu.VMEM((rows, depth, width, lanes), integrals.dtype),
-            pltpu.VMEM((group, share, cols * height), jnp.float32),
-            pltpu.VMEM((group - 1, share, cols * height), jnp.float32),
+            pltpu.VMEM((group,) + tile, jnp.float32),
+            pltpu.VMEM((group - 1,) + tile, jnp.float32),
             dma((max(cols - 1, 1), chunks)),
             dma((max(cols - 1, 1), chunks)),
             dma((max(rows - 1, 1), chunks)),

time: 49.4 us -> 48.8 us (0.988)
  Pallas kernels: 47.8 us -> 47.3 us
    pallas_call x1, Pallas kernels: 47.8 us -> 47.3 us  [local(): pl.pallas_call(functools.partial(kernel, sizes, split), out_shape=jax.Sha...]
where the time goes in v5:
time: 48.8 us; the launch traced here: 48.6 us
  Pallas kernels  47.3 us (97%)
  local copies, waits for them, and re-layouts  1.32 us (3%)
    pallas_call x1, Pallas kernels, local(): pl.pallas_call(functools.partial(kernel, sizes, split), out_shape=jax.Sha...  47.3 us
    unnamed x1, local copies, waits for them, and re-layouts  1.32 us

profile of v5, /device:TPU:0, one launch (start us, length us, event | category | flops | bytes accessed | tf_op | source)
XLA Modules:
  0.0 48.6 jit_solution(10795552387682979420)
XLA Ops:
  0.0 47.3 %shard_map.28 = f32[16,192]{1,0:T(8,128)} custom-call(bf16[25,48,1024]{2,1,0:T(8,128)(2,1)} %bitcast.2, bf16[25,256,128]{2,1,0:T(8,128)(2,1)} %b_ref.1), custom_call_target="tpu_custom_call" | custom-call | flops 629145600 | bytes 4096000 | tf_op jit(solution)/shard_map/pallas_call | solution.py:179
  47.3 1.3 %copy.4 = f32[192,16]{0,1:T(8,128)} copy(f32[192,16]{0,1:T(8,128)} %bitcast.3) | data formatting | bytes 24576

commit v6 on v5

--- a/solution.py
+++ b/solution.py
@@ -195,7 +195,7 @@
             dma((2,)),
         ],
         compiler_params=pltpu.CompilerParams(
-            collective_id=0, has_side_effects=True, vmem_limit_bytes=56 * 1024 * 1024),
+            collective_id=0, has_side_effects=True, vmem_limit_bytes=53 * 1024 * 1024),
         cost_estimate=pl.CostEstimate(
             flops=2 * cols * height * rows * lanes * depth * width,
             bytes_accessed=2 * (amplitudes.size + integrals.size), transcendentals=0),

time: 48.8 us -> 47.4 us (0.971)
  local copies, waits for them, and re-layouts: 1.32 us -> 0.61 us
  Pallas kernels: 47.3 us -> 46.7 us
    unnamed x1, local copies, waits for them, and re-layouts: 1.32 us -> 0.61 us
    pallas_call x1, Pallas kernels: 47.3 us -> 46.7 us  [local(): pl.pallas_call(functools.partial(kernel, sizes, split), out_shape=jax.Sha...]
where the time goes in v6:
time: 47.4 us; the launch traced here: 47.3 us
  Pallas kernels  46.7 us (99%)
  local copies, waits for them, and re-layouts  0.61 us (1%)
    pallas_call x1, Pallas kernels, local(): pl.pallas_call(functools.partial(kernel, sizes, split), out_shape=jax.Sha...  46.7 us

profile of v6, /device:TPU:0, one launch (start us, length us, event | category | flops | bytes accessed | tf_op | source)
XLA Modules:
  0.0 47.3 jit_solution(13381669287198838704)
XLA Ops:
  0.0 46.7 %shard_map.28 = f32[16,192]{1,0:T(8,128)S(1)} custom-call(bf16[25,48,1024]{2,1,0:T(8,128)(2,1)} %bitcast.3, bf16[25,256,128]{2,1,0:T(8,128)(2,1)} %b_ref.1), custom_call_target="tpu_custom_call" | custom-call | flops 629145600 | bytes 4096000 | tf_op jit(solution)/shard_map/pallas_call | solution.py:179
  46.7 0.6 %copy.4 = f32[192,16]{0,1:T(8,128)} copy(f32[192,16]{0,1:T(8,128)S(1)} %bitcast.2) | data formatting | bytes 24576

commit v7 on v6

--- a/solution.py
+++ b/solution.py
@@ -108,19 +108,22 @@
             device_id={"col": owner // reps, "rep": lax.rem(owner, reps)}, device_id_type=MESH)
 
     def hand_out(source, value):
-        if packed:
-            start = 0
-            for block in pack(value.T, per, share, full):
-                parts[pl.ds(source * per, per), start:start + block.shape[1]] = block
-                start += block.shape[1]
-        else:
-            parts[pl.ds(source * per, per)] = value.T.reshape(per, share, total_rows)
-        for i in range(per):
-            owner = source * per + i // reps * reps + lax.rem(2 * reps - 1 - rep - i % reps, reps)
-
-            @pl.when(owner != me)
-            def _():
-                part_copy(owner).start()
+        for first in range(0, per, reps):
+            block = value[:, first * share:(first + reps) * share].T
+            place = pl.ds(source * per + first, reps)
+            if packed:
+                start = 0
+                for part in pack(block, reps, share, full):
+                    parts[place, start:start + part.shape[1]] = part
+                    start += part.shape[1]
+            else:
+                parts[place] = block.reshape(reps, share, total_rows)
+            for i in range(reps):
+                owner = source * per + first + lax.rem(2 * reps - 1 - rep - i, reps)
+
+                @pl.when(owner != me)
+                def _():
+                    part_copy(owner).start()
 
     own_a.wait()
     own_b.wait()

time: 47.4 us -> 47.5 us (level)
  no operation moved by 1% of the time
where the time goes in v7:
time: 47.5 us; the launch traced here: 47.3 us
  Pallas kernels  46.7 us (98%)
  local copies, waits for them, and re-layouts  0.61 us (1%)
    pallas_call x1, Pallas kernels, local(): pl.pallas_call(functools.partial(kernel, sizes, split), out_shape=jax.Sha...  46.7 us

profile of v7, /device:TPU:0, one launch (start us, length us, event | category | flops | bytes accessed | tf_op | source)
XLA Modules:
  0.0 47.3 jit_solution(4362096362850869802)
XLA Ops:
  0.0 46.7 %shard_map.28 = f32[16,192]{1,0:T(8,128)S(1)} custom-call(bf16[25,48,1024]{2,1,0:T(8,128)(2,1)} %bitcast.3, bf16[25,256,128]{2,1,0:T(8,128)(2,1)} %b_ref.1), custom_call_target="tpu_custom_call" | custom-call | flops 629145600 | bytes 4096000 | tf_op jit(solution)/shard_map/pallas_call | solution.py:182
  46.7 0.6 %copy.4 = f32[192,16]{0,1:T(8,128)} copy(f32[192,16]{0,1:T(8,128)S(1)} %bitcast.2) | data formatting | bytes 24576
